TPU v7x, 32 devices: a whole 2x2x4 slice. The times are simulated.
32 devices in a mesh: seq: 8 (over z, x), tensor: 4 (over y, core).
Axes of the slice: x: 2, y: 2, z: 4, core: 2. Of those that a mesh axis runs over, the one named last changes fastest.
Arguments:
- queries: bfloat16 [7168, 2048], P('seq', 'tensor'), may hold values from -256 to 256
- db_states: bfloat16 [128, 64, 896], P('seq', None, 'tensor'), may hold values from -4096 to 4096
- enc_gain: float32 [896], replicated, may hold values from 0.1 to 1.9
- kv_weight: bfloat16 [896, 2, 2048], P(None, None, 'tensor'), may hold values from -0.1875 to 0.1875
- shard_ids: int32 [112, 2], P('seq'), may hold values from 0 to 7, as said below
- offsets: int32 [112, 2], P('seq'), may hold values from 0 to 14
Outputs:
- attention_out: bfloat16 [7168, 2048], P('seq', 'tensor')
Inputs may be any that keep to these rules, and one draw needn't show every extreme that they name: `shard_ids`: the neighbours named by the 14 groups of one device lie at most 4 in any one shard, and some shard is named exactly 4 times by the groups of every device.
All inputs are finite; a program needn't handle non-finite values.
Results may differ from a plain program's by a relative error of at most 0.0087.
Values may be sent and summed in bfloat16 or wider, within the bound.
A program may use at most 64 MiB of HBM per device.

v0:
```python
import math
import jax
import jax.numpy as jnp
from jax import lax
from jax.sharding import PartitionSpec as P

HEAD_DIM = 128
epsilon = 1e-06


def passed_along(block, axis, distance):
    devices = range(lax.axis_size(axis))
    route = [(i - distance, i) for i in devices if i - distance in devices]
    return lax.ppermute(block, axis, route)


def attend(query_win, kv_win):
    scores = jnp.einsum(
        "wqhd,wkhd->whqk", query_win, kv_win[:, :, 0], preferred_element_type=jnp.float32
    ) / math.sqrt(HEAD_DIM)
    highest = jnp.max(scores, axis=-1, keepdims=True)
    expo = jnp.exp(scores - highest)
    weights = (expo / jnp.sum(expo, axis=-1, keepdims=True)).astype(jnp.bfloat16)
    mixed = jnp.einsum(
        "whqk,wkhd->wqhd", weights, kv_win[:, :, 1], preferred_element_type=jnp.float32
    ).astype(jnp.bfloat16)
    return mixed.reshape(query_win.shape[0] * query_win.shape[1], -1)


def per_device(queries, db_states, enc_gain, kv_weight, shard_ids, offsets):
    seq_count = lax.axis_size("seq")
    group_count = shard_ids.shape[0]
    neigh_count = 2 * group_count
    slot_cap = (neigh_count + seq_count - 1) // seq_count
    group_len = db_states.shape[1]
    enc_width = kv_weight.shape[0]
    head_count = kv_weight.shape[2] // HEAD_DIM
    tok_count = queries.shape[0]
    query_cols = queries.shape[1]
    projection = kv_weight.reshape(enc_width, -1)
    token_rows = neigh_count * 2 * group_len
    neigh_shard = shard_ids.reshape(neigh_count)
    neigh_offset = offsets.reshape(neigh_count)
    owners = jnp.arange(seq_count, dtype=jnp.int32)
    onehot = (neigh_shard[:, None] == owners[None, :]).astype(jnp.int32)
    before = jnp.cumsum(onehot, axis=0) - onehot
    order_rank = jnp.sum(before * onehot, axis=1)
    slot_index = neigh_shard * slot_cap + order_rank
    table = jnp.zeros((seq_count * slot_cap,), jnp.int32).at[slot_index].set(neigh_offset + 1)
    wanted = lax.all_to_all(
        table.reshape(seq_count, slot_cap), "seq", split_axis=0, concat_axis=0, tiled=True
    )
    first_group = jnp.maximum(wanted - 1, 0)
    stored = db_states.reshape(db_states.shape[0], -1)
    outgoing = jnp.stack(
        [jnp.take(stored, first_group, axis=0), jnp.take(stored, first_group + 1, axis=0)], axis=2
    )
    incoming = lax.all_to_all(outgoing, "seq", split_axis=0, concat_axis=0, tiled=True)
    picked = jnp.take(incoming.reshape(seq_count * slot_cap, 2, -1), slot_index, axis=0)
    enc_rows = picked.reshape(token_rows, -1)
    as_float = lax.all_gather(enc_rows, "tensor", axis=1, tiled=True).astype(jnp.float32)
    scaled = (as_float * enc_gain[None, :]).astype(jnp.bfloat16)
    kv_sum = jnp.dot(scaled, projection, preferred_element_type=jnp.float32)
    kv_sum, square_sum = (kv_sum, jnp.sum(as_float * as_float, axis=1))
    inv_rms = lax.rsqrt(square_sum / enc_width + epsilon)
    keys_values = (kv_sum * inv_rms[:, None]).astype(jnp.bfloat16)
    kv_groups = keys_values.reshape(group_count, 4 * group_len, 2, head_count, HEAD_DIM)
    previous = passed_along(kv_groups[group_count - 1], "seq", 1)
    padded = jnp.concatenate(
        [
            jnp.zeros((1, query_cols), jnp.bfloat16),
            queries,
            jnp.zeros((group_len - 1, query_cols), jnp.bfloat16),
        ],
        axis=0,
    )
    windows = padded.reshape(group_count + 1, group_len, head_count, HEAD_DIM)
    attended = attend(windows, jnp.concatenate([previous[None], kv_groups], axis=0))
    result = attended[1 : tok_count + 1]
    return result


def solution(mesh):
    return jax.shard_map(
        per_device,
        mesh=mesh,
        in_specs=(
            P("seq", "tensor"),
            P("seq", None, "tensor"),
            P(),
            P(None, None, "tensor"),
            P("seq", None),
            P("seq", None),
        ),
        out_specs=P("seq", "tensor"),
        check_vma=False,
    )
```

profile of v0, /device:TPU:0, one launch (start us, length us, event | category | flops | bytes accessed | tf_op | source)
XLA Modules:
  0.0 213.9 jit_solution(16390059754301208129)
XLA Ops:
  6.5 0.7 broadcast_multiply_fusion
  7.2 0.8 copy.47
  8.0 0.7 broadcast_add_fusion
  10.8 7.3 %all-to-all-start = ((s32[8,1,4]{2,1,0:T(1,128)}), s32[8,1,4]{2,1,0:T(1,128)S(1)}, u32[]{:S(2)}, u32[]{:S(2)}) async-start(s32[8,1,4]{2,1,0:T(1,128)} %bitcast.2), calls=%async_computation | async-start | bytes 8192 | tf_op jit(solution)/shard_map/all_to_all | solution.py:50
  18.0 1.9 reshape.89
  20.0 4.5 %all-to-all-done = s32[8,1,4]{2,1,0:T(1,128)S(1)} async-done(((s32[8,1,4]{2,1,0:T(1,128)}), s32[8,1,4]{2,1,0:T(1,128)S(1)}, u32[]{:S(2)}, u32[]{:S(2)}) %all-to-all-start) | async-done | bytes 160 | tf_op jit(solution)/shard_map/all_to_all | solution.py:50
  25.1 1.1 gather_fusion.2
  26.5 1.1 gather_fusion.1
  28.0 0.9 select_bitcast_fusion
  28.9 2.5 %pad_maximum_fusion.1 = bf16[8,4,2,14336]{3,1,2,0:T(4,128)(2,1)} fusion(bf16[8,4,1,14336]{3,1,2,0:T(4,128)(2,1)S(1)} %get-tuple-element.10, bf16[8,4,1,14336]{3,1,2,0:T(4,128)(2,1)S(1)} %get-tuple-element.11), kind=kLoop, calls=%fused_computation.27 | loop fusion | flops 917504 | bytes 3670016 | tf_op jit(solution)/shard_map/stack | solution.py:55
  31.4 3.6 %all-to-all-start.1 = ((bf16[8,4,2,14336]{3,1,2,0:T(4,128)(2,1)}), bf16[8,4,2,14336]{3,1,2,0:T(4,128)(2,1)S(1)}, u32[]{:S(2)}, u32[]{:S(2)}) async-start(bf16[8,4,2,14336]{3,1,2,0:T(4,128)(2,1)} %pad_maximum_fusion.1), calls=%async_computation.1 | async-start | bytes 3670016 | tf_op jit(solution)/shard_map/all_to_all | solution.py:58
  35.3 41.1 %all-to-all-done.1 = bf16[8,4,2,14336]{3,1,2,0:T(4,128)(2,1)S(1)} async-done(((bf16[8,4,2,14336]{3,1,2,0:T(4,128)(2,1)}), bf16[8,4,2,14336]{3,1,2,0:T(4,128)(2,1)S(1)}, u32[]{:S(2)}, u32[]{:S(2)}) %all-to-all-start.1) | async-done | bytes 1835040 | tf_op jit(solution)/shard_map/all_to_all | solution.py:58
  76.4 3.1 %copy.56 = bf16[8,4,2,14336]{3,2,1,0:T(2,128)(2,1)} copy(bf16[8,4,2,14336]{3,1,2,0:T(4,128)(2,1)S(1)} %all-to-all-done.1) | data formatting | bytes 3670016 | tf_op jit(solution)/shard_map/all_to_all | solution.py:58
  79.5 5.3 %gather_fusion = bf16[28,2,14336]{2,1,0:T(2,128)(2,1)S(1)} fusion(bf16[32,2,14336]{2,1,0:T(2,128)(2,1)} %bitcast.48, s32[1024]{0:T(1024)S(1)} %pad_clamp_fusion), kind=kCustom, calls=%fused_computation.2 | custom fusion | bytes 3211376 | tf_op jit(solution)/shard_map/jit(_take)/gather | solution.py:59
  84.8 1.5 broadcast_select_fusion
  86.3 2.6 %select_n.35 = bf16[3584,224]{1,0:T(8,128)(2,1)S(1)} reshape(bf16[28,2,14336]{2,1,0:T(2,128)(2,1)S(1)} %broadcast_select_fusion) | data formatting | bytes 3211264 | tf_op jit(solution)/shard_map/jit(_take)/select_n | solution.py:59
  89.0 2.6 %copy.57 = bf16[3584,224]{0,1:T(8,128)(2,1)} copy(bf16[3584,224]{1,0:T(8,128)(2,1)S(1)} %select_n.35) | data formatting | bytes 3211264 | tf_op jit(solution)/shard_map/jit(_take)/select_n | solution.py:59
  91.6 2.0 copy.65
  93.6 44.3 %all-gather.2.cloned.1.call-done = bf16[3584,896]{0,1:T(8,128)(2,1)} async-done(((bf16[3584,224]{0,1:T(8,128)(2,1)}), bf16[3584,896]{0,1:T(8,128)(2,1)}) %all-gather.2.cloned.1.call-update) | async-done | bytes 6422544 | tf_op jit(solution)/shard_map/all_gather | solution.py:61
  137.9 4.3 %fusion.2 = f32[3584]{0:T(1024)S(1)} fusion(bf16[3584,896]{0,1:T(8,128)(2,1)} %all-gather.2.cloned.1.call-done), kind=kLoop, calls=%fused_computation.9 | loop fusion | flops 9630208 | bytes 6436864 | tf_op jit(solution)/shard_map/reduce_sum | solution.py:64
  142.5 8.7 %multiply_convert_fusion = bf16[3584,1024]{0,1:T(8,128)(2,1)S(1)} fusion(bf16[896,1024]{1,0:T(8,128)(2,1)S(1)} %bitcast.53, f32[3584]{0:T(1024)S(1)} %add_rsqrt_fusion, bf16[3584,896]{0,1:T(8,128)(2,1)S(1)} %copy-done.1, f32[896]{0:T(1024)S(1)} %copy-done.4), kind=kOutput, calls=%fused_computation.7 | convolution fusion | flops 6593642496 | bytes 15615488 | tf_op jit(solution)/shard_map/dot_general | solution.py:63
  151.2 3.0 %copy-done = bf16[3584,1024]{0,1:T(8,128)(2,1)} copy-done((bf16[3584,1024]{0,1:T(8,128)(2,1)}, bf16[3584,1024]{0,1:T(8,128)(2,1)S(1)}, u32[]{:S(2)}) %copy-start) | copy-done | bytes 7340056
  154.2 1.0 copy.58
  155.2 3.4 %collective-permute-start = (bf16[256,2,4,128]{3,0,2,1:T(8,128)(2,1)}, bf16[256,2,4,128]{3,0,2,1:T(8,128)(2,1)S(1)}, u32[]{:S(2)}, u32[]{:S(2)}) collective-permute-start(bf16[256,2,4,128]{3,0,2,1:T(8,128)(2,1)} %copy.58), channel_id=1, source_target_pairs={{0,4},{4,8},{8,12},{12,16},{16,20},{20,24},{24,28},{1,5},{5,9},{9,... | collective-permute-start | bytes 1572872 | tf_op jit(solution)/shard_map/ppermute | solution.py:14
  159.4 13.7 %reshape.139 = bf16[14,256,2,4,128]{1,0,4,3,2:T(8,128)(2,1)} reshape(bf16[3584,1024]{0,1:T(8,128)(2,1)} %copy-done) | data formatting | bytes 14680064 | tf_op jit(solution)/shard_map/reshape | solution.py:67
  173.1 14.2 %copy.60 = bf16[14,256,2,4,128]{4,1,3,0,2:T(8,128)(2,1)} copy(bf16[14,256,2,4,128]{1,0,4,3,2:T(8,128)(2,1)} %reshape.139) | data formatting | bytes 14680064 | tf_op jit(solution)/shard_map/reshape | solution.py:67
  187.3 3.1 %fusion.7 = f32[15,4,64,256]{3,2,1,0:T(8,128)S(1)} fusion(bf16[1,256,2,4,128]{4,1,3,0,2:T(8,128)(2,1)S(1)} %bitcast.54, bf16[14,256,2,4,128]{4,1,3,0,2:T(8,128)(2,1)} %copy.60, bf16[15,64,4,128]{3,2,1,0:T(4,128)(2,1)S(1)} %reshape.93), kind=kOutput, calls=%fused_computation.15 | convolution fusion | flops 253624320 | bytes 12779520 | tf_op jit(solution)/shard_map/wqhd,wkhd->whqk/dot_general | solution.py:18
  190.4 1.9 copy-done.2
  192.3 1.5 fusion.39
  193.7 11.2 %fusion.21 = bf16[15,64,4,128]{3,1,2,0:T(8,128)(2,1)S(1)} fusion(bf16[14,256,2,4,128]{4,1,3,0,2:T(8,128)(2,1)} %copy.60, bf16[1,256,2,4,128]{4,1,3,0,2:T(8,128)(2,1)S(1)} %bitcast.55, f32[15,4,64]{2,1,0:T(4,128)S(1)} %fusion.39, f32[15,4,64,256]{3,2,1,0:T(8,128)} %copy-done.2), kind=kOutput, calls=%fused_computation.29 | convolution fusion | flops 264933376 | bytes 12794880 | tf_op jit(solution)/shard_map/whqk,wkhd->wqhd/dot_general | solution.py:24
  204.9 0.8 copy.62
  205.9 1.1 slice.26
  (45 shorter events, 5.0 us)
Async XLA Ops:
  10.8 13.6 %all-to-all-start = ((s32[8,1,4]{2,1,0:T(1,128)}), s32[8,1,4]{2,1,0:T(1,128)S(1)}, u32[]{:S(2)}, u32[]{:S(2)}) async-start(s32[8,1,4]{2,1,0:T(1,128)} %bitcast.2), calls=%async_computation | async-start | bytes 8192 | tf_op jit(solution)/shard_map/all_to_all | solution.py:50
  31.4 45.0 %all-to-all-start.1 = ((bf16[8,4,2,14336]{3,1,2,0:T(4,128)(2,1)}), bf16[8,4,2,14336]{3,1,2,0:T(4,128)(2,1)S(1)}, u32[]{:S(2)}, u32[]{:S(2)}) async-start(bf16[8,4,2,14336]{3,1,2,0:T(4,128)(2,1)} %pad_maximum_fusion.1), calls=%async_computation.1 | async-start | bytes 3670016 | tf_op jit(solution)/shard_map/all_to_all | solution.py:58
  35.0 102.9 %all-gather.2.cloned.1.call-start = ((), (), s32[]{:S(2)}) async-start(), calls=%async_computation.2 | async-start | bytes 8028160 | tf_op jit(solution)/shard_map/all_gather | solution.py:61
  93.6 48.6 %copy-start.4 = (f32[896]{0:T(1024)S(1)}, f32[896]{0:T(1024)}, u32[]{:S(2)}) copy-start(f32[896]{0:T(1024)} %param.10) | copy-start | bytes 10756
  137.9 4.7 %copy-start.1 = (bf16[3584,896]{0,1:T(8,128)(2,1)S(1)}, bf16[3584,896]{0,1:T(8,128)(2,1)}, u32[]{:S(2)}) copy-start(bf16[3584,896]{0,1:T(8,128)(2,1)} %all-gather.2.cloned.1.call-done) | copy-start | bytes 19267588
  142.5 16.2 %copy-start.3 = (bf16[896,512]{1,0:T(8,128)(2,1)S(1)}, bf16[896,512]{1,0:T(8,128)(2,1)}, u32[]{:S(2)}) copy-start(bf16[896,512]{1,0:T(8,128)(2,1)} %param.8) | copy-start | bytes 2752516
  151.2 3.0 %copy-start = (bf16[3584,1024]{0,1:T(8,128)(2,1)}, bf16[3584,1024]{0,1:T(8,128)(2,1)S(1)}, u32[]{:S(2)}) copy-start(bf16[3584,1024]{0,1:T(8,128)(2,1)S(1)} %multiply_convert_fusion) | copy-start | bytes 22020100
  155.2 32.0 %collective-permute-start = (bf16[256,2,4,128]{3,0,2,1:T(8,128)(2,1)}, bf16[256,2,4,128]{3,0,2,1:T(8,128)(2,1)S(1)}, u32[]{:S(2)}, u32[]{:S(2)}) collective-permute-start(bf16[256,2,4,128]{3,0,2,1:T(8,128)(2,1)} %copy.58), channel_id=1, source_target_pairs={{0,4},{4,8},{8,12},{12,16},{16,20},{20,24},{24,28},{1,5},{5,9},{9,... | collective-permute-start | bytes 1572872 | tf_op jit(solution)/shard_map/ppermute | solution.py:14
  190.4 1.9 copy-start.2
Sparse Core Ops, SparseCore 0:
  91.7 46.1 all-gather.1
where the time goes:
time: 215 us; the launch traced here: 214 us
  waiting for transfers between devices  89.9 us (42%)
  local copies, waits for them, and re-layouts  60.2 us (28%)
  matrix products  23 us (11%)
  starting transfers between devices  14.4 us (7%)
  between operations  13.6 us (6%)
  other arithmetic  12.7 us (6%)
    all_gather x1, waiting for transfers between devices, per_device(): lax.all_gather(enc_rows, 'tensor', axis=1, tiled=True).astype(jnp.float32)  44.3 us
    all_to_all x1, waiting for transfers between devices, per_device(): lax.all_to_all(outgoing, 'seq', split_axis=0, concat_axis=0, tiled=True)  41.1 us
    reshape x2, local copies, waits for them, and re-layouts, per_device(): keys_values.reshape(group_count, 4 * group_len, 2, head_count, HEAD_DIM)  27.9 us
    dot_general x1, matrix products, attend(): jnp.einsum('whqk,wkhd->wqhd', weights, kv_win[:, :, 1], preferred_element...  11.2 us
    dot_general x1, matrix products, per_device(): kv_sum = jnp.dot(scaled, projection, preferred_element_type=jnp.float32)  8.67 us
    unnamed x13, local copies, waits for them, and re-layouts  8.17 us
    all_to_all x1, starting transfers between devices, per_device(): lax.all_to_all(table.reshape(seq_count, slot_cap), 'seq', split_axis=0, c...  7.25 us
    gather x1, local copies, waits for them, and re-layouts, per_device(): jnp.take(incoming.reshape(seq_count * slot_cap, 2, -1), slot_index, axis=0)  5.28 us
  transfers between devices with their start and end apart: 4, of which 3 were waited for; matrix products, arithmetic and copies ran while one was open for 15% of the time, Pallas kernels for 0%

commit v1 on v0

--- a/solution.py
+++ b/solution.py
@@ -1,3 +1,4 @@
+import functools
 import math
 import jax
 import jax.numpy as jnp
@@ -6,6 +7,32 @@
 
 HEAD_DIM = 128
 epsilon = 1e-06
+
+
+def list_the_sectors(z, d0, ndim_at):
+    x_new, z2 = (jax.lax.axis_size("seq"), jax.lax.axis_index("seq"))
+    frame_out = list(z.shape)
+    big = z.shape[ndim_at] // x_new
+    frame_out[ndim_at] = big
+    m_next = frame_out[d0]
+    frame_out[d0] = m_next * x_new
+    plain = jnp.zeros(frame_out, z.dtype)
+    q = 0
+    while q < x_new:
+        tile_out = lax.dynamic_slice_in_dim(z, (z2 ^ q) * big, big, axis=ndim_at)
+        if q:
+            kept_rows = []
+            nth = 0
+            while nth < x_new:
+                kept_rows.append((nth, nth ^ q))
+                nth += 1
+            tile_out = jax.lax.ppermute(tile_out, "seq", kept_rows)
+        plain = lax.dynamic_update_slice_in_dim(plain, tile_out, (z2 ^ q) * m_next, axis=d0)
+        q += 1
+    return plain
+
+
+begin_tails = functools.partial(list_the_sectors, d0=0, ndim_at=0)
 
 
 def passed_along(block, axis, distance):
@@ -55,7 +82,7 @@
     outgoing = jnp.stack(
         [jnp.take(stored, first_group, axis=0), jnp.take(stored, first_group + 1, axis=0)], axis=2
     )
-    incoming = lax.all_to_all(outgoing, "seq", split_axis=0, concat_axis=0, tiled=True)
+    incoming = begin_tails(outgoing)
     picked = jnp.take(incoming.reshape(seq_count * slot_cap, 2, -1), slot_index, axis=0)
     enc_rows = picked.reshape(token_rows, -1)
     as_float = lax.all_gather(enc_rows, "tensor", axis=1, tiled=True).astype(jnp.float32)

time: 215 us -> 207 us (0.963)
  waiting for transfers between devices: 89.9 us -> 71 us
  starting transfers between devices: 14.4 us -> 24.8 us
    all_to_all x1 -> x0, waiting for transfers between devices: 41.1 us -> none  [per_device(): lax.all_to_all(outgoing, 'seq', split_axis=0, concat_axis=0, tiled=True)]
    ppermute x0 -> x7, waiting for transfers between devices: none -> 23.2 us  [list_the_sectors(): tile_out = jax.lax.ppermute(tile_out, 'seq', kept_rows)]
    ppermute x0 -> x7, starting transfers between devices: none -> 13.9 us  [list_the_sectors(): tile_out = jax.lax.ppermute(tile_out, 'seq', kept_rows)]
    all_to_all x1 -> x0, starting transfers between devices: 3.59 us -> none  [per_device(): lax.all_to_all(outgoing, 'seq', split_axis=0, concat_axis=0, tiled=True)]
    all_to_all x1 -> x0, local copies, waits for them, and re-layouts: 3.14 us -> none  [per_device(): lax.all_to_all(outgoing, 'seq', split_axis=0, concat_axis=0, tiled=True)]
  transfers between devices with their start and end apart: 4 -> 10, of which waited for: 3 -> 6; matrix products, arithmetic and copies ran while one was open for 15% -> 18% of each run, Pallas kernels for 0% -> 0%
where the time goes in v1:
time: 207 us; the launch traced here: 206 us
  waiting for transfers between devices  71 us (34%)
  local copies, waits for them, and re-layouts  60.7 us (29%)
  starting transfers between devices  24.8 us (12%)
  matrix products  22.9 us (11%)
  between operations  13.8 us (7%)
  other arithmetic  12.8 us (6%)
    all_gather x1, waiting for transfers between devices, per_device(): lax.all_gather(enc_rows, 'tensor', axis=1, tiled=True).astype(jnp.float32)  43.5 us
    reshape x2, local copies, waits for them, and re-layouts, per_device(): keys_values.reshape(group_count, 4 * group_len, 2, head_count, HEAD_DIM)  27.6 us
    ppermute x7, waiting for transfers between devices, list_the_sectors(): tile_out = jax.lax.ppermute(tile_out, 'seq', kept_rows)  23.2 us
    ppermute x7, starting transfers between devices, list_the_sectors(): tile_out = jax.lax.ppermute(tile_out, 'seq', kept_rows)  13.9 us
    dot_general x1, matrix products, attend(): jnp.einsum('whqk,wkhd->wqhd', weights, kv_win[:, :, 1], preferred_element...  11.2 us
    dot_general x1, matrix products, per_device(): kv_sum = jnp.dot(scaled, projection, preferred_element_type=jnp.float32)  8.67 us
    unnamed x13, local copies, waits for them, and re-layouts  8.14 us
    select_n x2, local copies, waits for them, and re-layouts, per_device(): jnp.take(incoming.reshape(seq_count * slot_cap, 2, -1), slot_index, axis=0)  7.28 us
  transfers between devices with their start and end apart: 10, of which 6 were waited for; matrix products, arithmetic and copies ran while one was open for 18% of the time, Pallas kernels for 0%

profile of v1, /device:TPU:0, one launch (start us, length us, event | category | flops | bytes accessed | tf_op | source)
XLA Modules:
  0.0 206.0 jit_solution(6116577742345557067)
XLA Ops:
  10.8 7.3 %all-to-all-start = ((s32[8,1,4]{2,1,0:T(1,128)}), s32[8,1,4]{2,1,0:T(1,128)S(1)}, u32[]{:S(2)}, u32[]{:S(2)}) async-start(s32[8,1,4]{2,1,0:T(1,128)} %bitcast.2), calls=%async_computation | async-start | bytes 8192 | tf_op jit(solution)/shard_map/all_to_all | solution.py:77
  18.1 1.9 reshape.89
  20.1 4.3 %all-to-all-done = s32[8,1,4]{2,1,0:T(1,128)S(1)} async-done(((s32[8,1,4]{2,1,0:T(1,128)}), s32[8,1,4]{2,1,0:T(1,128)S(1)}, u32[]{:S(2)}, u32[]{:S(2)}) %all-to-all-start) | async-done | bytes 160 | tf_op jit(solution)/shard_map/all_to_all | solution.py:77
  25.1 1.1 gather_fusion.2
  26.5 1.1 gather_fusion.1
  29.9 1.5 collective-permute-start.4
  31.3 1.1 fusion.25
  32.4 2.4 %collective-permute-start.6 = (bf16[1,4,2,14336]{3,1,0,2:T(4,128)(2,1)S(1)}, bf16[1,4,2,14336]{3,1,0,2:T(4,128)(2,1)S(1)}, u32[]{:S(2)}, u32[]{:S(2)}) collective-permute-start(bf16[1,4,2,14336]{3,1,0,2:T(4,128)(2,1)S(1)} %get-tuple-element.6), channel_id=1, source_target_pairs={{0,28},{4,24},{8,20},{12,16},{16,12},{20,8},{24,4},{28,0},{1,29},{... | collective-permute-start | bytes 688136 | tf_op jit(solution)/shard_map/ppermute | solution.py:29
  36.4 1.2 broadcast_in_dim.41
  37.8 4.4 %collective-permute-done = bf16[1,4,2,14336]{3,1,0,2:T(4,128)(2,1)S(1)} collective-permute-done((bf16[1,4,2,14336]{3,1,0,2:T(4,128)(2,1)S(1)}, bf16[1,4,2,14336]{3,1,0,2:T(4,128)(2,1)S(1)}, u32[]{:S(2)}, u32[]{:S(2)}) %collective-permute-start) | collective-permute-done | bytes 229408 | tf_op jit(solution)/shard_map/ppermute | solution.py:29
  42.3 3.6 %collective-permute-start.2 = (bf16[1,4,2,14336]{3,1,0,2:T(4,128)(2,1)S(1)}, bf16[1,4,2,14336]{3,1,0,2:T(4,128)(2,1)S(1)}, u32[]{:S(2)}, u32[]{:S(2)}) collective-permute-start(bf16[1,4,2,14336]{3,1,0,2:T(4,128)(2,1)S(1)} %get-tuple-element.10), channel_id=1, source_target_pairs={{0,12},{4,8},{8,4},{12,0},{16,28},{20,24},{24,20},{28,16},{1,13},{... | collective-permute-start | bytes 688136 | tf_op jit(solution)/shard_map/ppermute | solution.py:29
  46.1 4.6 %collective-permute-done.1 = bf16[1,4,2,14336]{3,1,0,2:T(4,128)(2,1)S(1)} collective-permute-done((bf16[1,4,2,14336]{3,1,0,2:T(4,128)(2,1)S(1)}, bf16[1,4,2,14336]{3,1,0,2:T(4,128)(2,1)S(1)}, u32[]{:S(2)}, u32[]{:S(2)}) %collective-permute-start.1) | collective-permute-done | bytes 229408 | tf_op jit(solution)/shard_map/ppermute | solution.py:29
  50.7 4.3 %collective-permute-start.3 = (bf16[1,4,2,14336]{3,1,0,2:T(4,128)(2,1)S(1)}, bf16[1,4,2,14336]{3,1,0,2:T(4,128)(2,1)S(1)}, u32[]{:S(2)}, u32[]{:S(2)}) collective-permute-start(bf16[1,4,2,14336]{3,1,0,2:T(4,128)(2,1)S(1)} %get-tuple-element.11), channel_id=1, source_target_pairs={{0,16},{4,20},{8,24},{12,28},{16,0},{20,4},{24,8},{28,12},{1,17},{... | collective-permute-start | bytes 688136 | tf_op jit(solution)/shard_map/ppermute | solution.py:29
  55.2 1.7 collective-permute-done.2
  57.2 12.4 %collective-permute-done.3 = bf16[1,4,2,14336]{3,1,0,2:T(4,128)(2,1)S(1)} collective-permute-done((bf16[1,4,2,14336]{3,1,0,2:T(4,128)(2,1)S(1)}, bf16[1,4,2,14336]{3,1,0,2:T(4,128)(2,1)S(1)}, u32[]{:S(2)}, u32[]{:S(2)}) %collective-permute-start.3) | collective-permute-done | bytes 229408 | tf_op jit(solution)/shard_map/ppermute | solution.py:29
  70.7 4.0 %gather_fusion = bf16[28,2,14336]{2,1,0:T(2,128)(2,1)S(1)} fusion(bf16[32,2,14336]{2,1,0:T(2,128)(2,1)S(1)} %bitcast.48, s32[1024]{0:T(1024)S(1)} %pad_clamp_fusion), kind=kCustom, calls=%fused_computation.2 | custom fusion | bytes 3211376 | tf_op jit(solution)/shard_map/jit(_take)/gather | solution.py:86
  74.7 2.7 %broadcast_select_fusion = bf16[28,2,14336]{2,1,0:T(2,128)(2,1)} fusion(bf16[28,2,14336]{2,1,0:T(2,128)(2,1)S(1)} %gather_fusion, pred[28]{0:T(512)(128)(4,1)S(1)} %compare_and_fusion.2), kind=kLoop, calls=%fused_computation.24 | loop fusion | flops 802816 | bytes 3211292 | tf_op jit(solution)/shard_map/jit(_take)/select_n | solution.py:86
  77.3 4.7 %select_n.75 = bf16[3584,224]{1,0:T(8,128)(2,1)S(1)} reshape(bf16[28,2,14336]{2,1,0:T(2,128)(2,1)} %broadcast_select_fusion) | data formatting | bytes 3211264 | tf_op jit(solution)/shard_map/jit(_take)/select_n | solution.py:86
  82.0 2.6 %copy.78 = bf16[3584,224]{0,1:T(8,128)(2,1)} copy(bf16[3584,224]{1,0:T(8,128)(2,1)S(1)} %select_n.75) | data formatting | bytes 3211264 | tf_op jit(solution)/shard_map/jit(_take)/select_n | solution.py:86
  84.6 2.0 copy.86
  86.6 43.5 %all-gather.2.cloned.1.call-done = bf16[3584,896]{0,1:T(8,128)(2,1)} async-done(((bf16[3584,224]{0,1:T(8,128)(2,1)}), bf16[3584,896]{0,1:T(8,128)(2,1)}) %all-gather.2.cloned.1.call-update) | async-done | bytes 6422544 | tf_op jit(solution)/shard_map/all_gather | solution.py:88
  130.1 4.3 %fusion.2 = f32[3584]{0:T(1024)S(1)} fusion(bf16[3584,896]{0,1:T(8,128)(2,1)} %all-gather.2.cloned.1.call-done), kind=kLoop, calls=%fused_computation.9 | loop fusion | flops 9630208 | bytes 6436864 | tf_op jit(solution)/shard_map/reduce_sum | solution.py:91
  134.8 8.7 %multiply_convert_fusion = bf16[3584,1024]{0,1:T(8,128)(2,1)S(1)} fusion(bf16[896,1024]{1,0:T(8,128)(2,1)S(1)} %bitcast.53, f32[3584]{0:T(1024)S(1)} %add_rsqrt_fusion, bf16[3584,896]{0,1:T(8,128)(2,1)S(1)} %copy-done.1, f32[896]{0:T(1024)S(1)} %copy-done.4), kind=kOutput, calls=%fused_computation.7 | convolution fusion | flops 6593642496 | bytes 15615488 | tf_op jit(solution)/shard_map/dot_general | solution.py:90
  143.5 3.0 %copy-done = bf16[3584,1024]{0,1:T(8,128)(2,1)} copy-done((bf16[3584,1024]{0,1:T(8,128)(2,1)}, bf16[3584,1024]{0,1:T(8,128)(2,1)S(1)}, u32[]{:S(2)}) %copy-start) | copy-done | bytes 7340056
  147.5 3.6 %collective-permute-start.7 = (bf16[256,2,4,128]{3,0,2,1:T(8,128)(2,1)}, bf16[256,2,4,128]{3,0,2,1:T(8,128)(2,1)S(1)}, u32[]{:S(2)}, u32[]{:S(2)}) collective-permute-start(bf16[256,2,4,128]{3,0,2,1:T(8,128)(2,1)} %copy.79), channel_id=1, source_target_pairs={{0,4},{4,8},{8,12},{12,16},{16,20},{20,24},{24,28},{1,5},{5,9},{9,... | collective-permute-start | bytes 1572872 | tf_op jit(solution)/shard_map/ppermute | solution.py:41
  151.8 13.5 %reshape.139 = bf16[14,256,2,4,128]{1,0,4,3,2:T(8,128)(2,1)} reshape(bf16[3584,1024]{0,1:T(8,128)(2,1)} %copy-done) | data formatting | bytes 14680064 | tf_op jit(solution)/shard_map/reshape | solution.py:94
  165.3 14.2 %copy.81 = bf16[14,256,2,4,128]{4,1,3,0,2:T(8,128)(2,1)} copy(bf16[14,256,2,4,128]{1,0,4,3,2:T(8,128)(2,1)} %reshape.139) | data formatting | bytes 14680064 | tf_op jit(solution)/shard_map/reshape | solution.py:94
  179.5 3.1 %fusion.7 = f32[15,4,64,256]{3,2,1,0:T(8,128)S(1)} fusion(bf16[1,256,2,4,128]{4,1,3,0,2:T(8,128)(2,1)S(1)} %bitcast.54, bf16[14,256,2,4,128]{4,1,3,0,2:T(8,128)(2,1)} %copy.81, bf16[15,64,4,128]{3,2,1,0:T(4,128)(2,1)S(1)} %reshape.93), kind=kOutput, calls=%fused_computation.15 | convolution fusion | flops 253624320 | bytes 12779520 | tf_op jit(solution)/shard_map/wqhd,wkhd->whqk/dot_general | solution.py:45
  182.6 1.8 copy-done.2
  184.4 1.5 fusion.47
  185.9 11.2 %fusion.21 = bf16[15,64,4,128]{3,1,2,0:T(8,128)(2,1)S(1)} fusion(bf16[14,256,2,4,128]{4,1,3,0,2:T(8,128)(2,1)} %copy.81, bf16[1,256,2,4,128]{4,1,3,0,2:T(8,128)(2,1)S(1)} %bitcast.55, f32[15,4,64]{2,1,0:T(4,128)S(1)} %fusion.47, f32[15,4,64,256]{3,2,1,0:T(8,128)} %copy-done.2), kind=kOutput, calls=%fused_computation.44 | convolution fusion | flops 264933376 | bytes 12794880 | tf_op jit(solution)/shard_map/whqk,wkhd->wqhd/dot_general | solution.py:51
  198.1 1.1 slice.26
  (66 shorter events, 14.2 us)
Async XLA Ops:
  10.8 13.6 %all-to-all-start = ((s32[8,1,4]{2,1,0:T(1,128)}), s32[8,1,4]{2,1,0:T(1,128)S(1)}, u32[]{:S(2)}, u32[]{:S(2)}) async-start(s32[8,1,4]{2,1,0:T(1,128)} %bitcast.2), calls=%async_computation | async-start | bytes 8192 | tf_op jit(solution)/shard_map/all_to_all | solution.py:77
  18.0 112.1 %all-gather.2.cloned.1.call-start = ((), (), s32[]{:S(2)}) async-start(), calls=%async_computation.1 | async-start | bytes 8028160 | tf_op jit(solution)/shard_map/all_gather | solution.py:88
  29.2 40.9 %collective-permute-start.5 = (bf16[1,4,2,14336]{3,1,0,2:T(4,128)(2,1)S(1)}, bf16[1,4,2,14336]{3,1,0,2:T(4,128)(2,1)S(1)}, u32[]{:S(2)}, u32[]{:S(2)}) collective-permute-start(bf16[1,4,2,14336]{3,1,0,2:T(4,128)(2,1)S(1)} %get-tuple-element.12), channel_id=1, source_target_pairs={{0,24},{4,28},{8,16},{12,20},{16,8},{20,12},{24,0},{28,4},{1,25},{... | collective-permute-start | bytes 688136 | tf_op jit(solution)/shard_map/ppermute | solution.py:29
  29.9 40.0 %collective-permute-start.4 = (bf16[1,4,2,14336]{3,1,0,2:T(4,128)(2,1)S(1)}, bf16[1,4,2,14336]{3,1,0,2:T(4,128)(2,1)S(1)}, u32[]{:S(2)}, u32[]{:S(2)}) collective-permute-start(bf16[1,4,2,14336]{3,1,0,2:T(4,128)(2,1)S(1)} %get-tuple-element.13), channel_id=1, source_target_pairs={{0,20},{4,16},{8,28},{12,24},{16,4},{20,0},{24,12},{28,8},{1,21},{... | collective-permute-start | bytes 688136 | tf_op jit(solution)/shard_map/ppermute | solution.py:29
  32.4 38.0 %collective-permute-start.6 = (bf16[1,4,2,14336]{3,1,0,2:T(4,128)(2,1)S(1)}, bf16[1,4,2,14336]{3,1,0,2:T(4,128)(2,1)S(1)}, u32[]{:S(2)}, u32[]{:S(2)}) collective-permute-start(bf16[1,4,2,14336]{3,1,0,2:T(4,128)(2,1)S(1)} %get-tuple-element.6), channel_id=1, source_target_pairs={{0,28},{4,24},{8,20},{12,16},{16,12},{20,8},{24,4},{28,0},{1,29},{... | collective-permute-start | bytes 688136 | tf_op jit(solution)/shard_map/ppermute | solution.py:29
  34.8 7.4 %collective-permute-start = (bf16[1,4,2,14336]{3,1,0,2:T(4,128)(2,1)S(1)}, bf16[1,4,2,14336]{3,1,0,2:T(4,128)(2,1)S(1)}, u32[]{:S(2)}, u32[]{:S(2)}) collective-permute-start(bf16[1,4,2,14336]{3,1,0,2:T(4,128)(2,1)S(1)} %get-tuple-element.8), channel_id=1, source_target_pairs={{0,4},{4,0},{8,12},{12,8},{16,20},{20,16},{24,28},{28,24},{1,5},{5... | collective-permute-start | bytes 688136 | tf_op jit(solution)/shard_map/ppermute | solution.py:29
  35.8 14.9 %collective-permute-start.1 = (bf16[1,4,2,14336]{3,1,0,2:T(4,128)(2,1)S(1)}, bf16[1,4,2,14336]{3,1,0,2:T(4,128)(2,1)S(1)}, u32[]{:S(2)}, u32[]{:S(2)}) collective-permute-start(bf16[1,4,2,14336]{3,1,0,2:T(4,128)(2,1)S(1)} %get-tuple-element.9), channel_id=1, source_target_pairs={{0,8},{4,12},{8,0},{12,4},{16,24},{20,28},{24,16},{28,20},{1,9},{5... | collective-permute-start | bytes 688136 | tf_op jit(solution)/shard_map/ppermute | solution.py:29
  42.3 14.7 %collective-permute-start.2 = (bf16[1,4,2,14336]{3,1,0,2:T(4,128)(2,1)S(1)}, bf16[1,4,2,14336]{3,1,0,2:T(4,128)(2,1)S(1)}, u32[]{:S(2)}, u32[]{:S(2)}) collective-permute-start(bf16[1,4,2,14336]{3,1,0,2:T(4,128)(2,1)S(1)} %get-tuple-element.10), channel_id=1, source_target_pairs={{0,12},{4,8},{8,4},{12,0},{16,28},{20,24},{24,20},{28,16},{1,13},{... | collective-permute-start | bytes 688136 | tf_op jit(solution)/shard_map/ppermute | solution.py:29
  50.7 18.9 %collective-permute-start.3 = (bf16[1,4,2,14336]{3,1,0,2:T(4,128)(2,1)S(1)}, bf16[1,4,2,14336]{3,1,0,2:T(4,128)(2,1)S(1)}, u32[]{:S(2)}, u32[]{:S(2)}) collective-permute-start(bf16[1,4,2,14336]{3,1,0,2:T(4,128)(2,1)S(1)} %get-tuple-element.11), channel_id=1, source_target_pairs={{0,16},{4,20},{8,24},{12,28},{16,0},{20,4},{24,8},{28,12},{1,17},{... | collective-permute-start | bytes 688136 | tf_op jit(solution)/shard_map/ppermute | solution.py:29
  86.6 47.8 %copy-start.4 = (f32[896]{0:T(1024)S(1)}, f32[896]{0:T(1024)}, u32[]{:S(2)}) copy-start(f32[896]{0:T(1024)} %param.10) | copy-start | bytes 10756
  130.1 4.7 %copy-start.1 = (bf16[3584,896]{0,1:T(8,128)(2,1)S(1)}, bf16[3584,896]{0,1:T(8,128)(2,1)}, u32[]{:S(2)}) copy-start(bf16[3584,896]{0,1:T(8,128)(2,1)} %all-gather.2.cloned.1.call-done) | copy-start | bytes 19267588
  143.5 3.0 %copy-start = (bf16[3584,1024]{0,1:T(8,128)(2,1)}, bf16[3584,1024]{0,1:T(8,128)(2,1)S(1)}, u32[]{:S(2)}) copy-start(bf16[3584,1024]{0,1:T(8,128)(2,1)S(1)} %multiply_convert_fusion) | copy-start | bytes 22020100
  146.5 4.7 %copy-start.3 = (bf16[896,512]{1,0:T(8,128)(2,1)S(1)}, bf16[896,512]{1,0:T(8,128)(2,1)}, u32[]{:S(2)}) copy-start(bf16[896,512]{1,0:T(8,128)(2,1)} %param.8) | copy-start | bytes 2752516
  147.5 32.0 %collective-permute-start.7 = (bf16[256,2,4,128]{3,0,2,1:T(8,128)(2,1)}, bf16[256,2,4,128]{3,0,2,1:T(8,128)(2,1)S(1)}, u32[]{:S(2)}, u32[]{:S(2)}) collective-permute-start(bf16[256,2,4,128]{3,0,2,1:T(8,128)(2,1)} %copy.79), channel_id=1, source_target_pairs={{0,4},{4,8},{8,12},{12,16},{16,20},{20,24},{24,28},{1,5},{5,9},{9,... | collective-permute-start | bytes 1572872 | tf_op jit(solution)/shard_map/ppermute | solution.py:41
  182.6 1.9 copy-start.2
Sparse Core Ops, SparseCore 0:
  84.7 45.3 all-gather.1
